TPU v7x, 32 devices: a whole 2x2x4 slice. The times are simulated.
32 devices in a mesh: fsdp: 8 (over y, x, core), cp: 4 (over z).
Axes of the slice: x: 2, y: 2, z: 4, core: 2. Of those that a mesh axis runs over, the one named last changes fastest.
Arguments:
- queries: bfloat16 [1024, 4096], P('cp', 'fsdp'), may hold values from -8 to 8
- key_vectors: bfloat16 [1024, 256], P(('fsdp', 'cp')), may hold values from -8 to 8
- value_vectors: bfloat16 [1024, 256], P(('fsdp', 'cp')), may hold values from -6 to 6
- out_grads: bfloat16 [1024, 4096], P('cp', 'fsdp'), may hold values from -6 to 6
- pair_order: int32 [8], replicated, may hold values from 0 to 7, as said below
Outputs:
- attended: bfloat16 [1024, 4096], P('cp', 'fsdp')
- query_grads: bfloat16 [1024, 4096], P('cp', 'fsdp')
- key_grads: float32 [1024, 256], P(('fsdp', 'cp'))
- value_grads: float32 [1024, 256], P(('fsdp', 'cp'))
Inputs may be any that keep to these rules, and one draw needn't show every extreme that they name: `pair_order`: A permutation of the stretches; slots 2 c and 2 c + 1 hold stretches P and 7 - P for some P, in either order.
All inputs are finite; a program needn't handle non-finite values.
Results may differ from a plain program's by a relative error of at most 0.034.
Values may be sent and summed in bfloat16 or wider, within the bound.
A program may use at most 64 MiB of HBM per device.

v0:
```python
import functools
import math

import jax
import jax.numpy as jnp
from jax import lax
from jax.experimental import pallas as pl
from jax.experimental.pallas import tpu as pltpu
from jax.sharding import PartitionSpec as P

HD = 128
NEG_FILL = -1e30
F32 = jnp.float32
BF16 = jnp.bfloat16


def rows_of(blocks, count):
    if blocks.shape[-2] % 16 == 0:
        return blocks.reshape(count, HD)
    return blocks.astype(F32).reshape(count, HD).astype(BF16)


def dot_nt(left, right):
    return lax.dot_general(left, right, (((1,), (1,)), ((), ())), preferred_element_type=F32)


def dot_nn(left, right):
    return lax.dot_general(left, right, (((1,), (0,)), ((), ())), preferred_element_type=F32)


def run_steps(low, high, step):
    if high - low <= 4:
        for i in range(low, high):
            step(i)
    else:
        lax.fori_loop(low, high, lambda i, carry: (step(i), carry)[1], 0)


def kernel(
    F,
    C,
    G,
    order_ref,
    q_in,
    k_in,
    v_in,
    do_in,
    o_out,
    dq_out,
    dk_out,
    dv_out,
    q_ref,
    k_ref,
    v_ref,
    do_ref,
    o_ref,
    dq_ref,
    dk_ref,
    dv_ref,
    in_sem,
    out_sem,
    cp_buf,
    kv_buf,
    send_buf,
    twin_buf,
    pair_buf,
    r1_buf,
    r2_send,
    r2_buf,
    kt_buf,
    dot_buf,
    s_buf,
    dp_buf,
    peak_buf,
    total_buf,
    outt_buf,
    seen_buf,
    delta_buf,
    dqt_buf,
    send1,
    recv1,
    send2,
    recv2,
    send3,
    recv3,
    send4,
    recv4,
    twin_send,
    twin_recv,
    pair_send,
    pair_recv,
):
    f = lax.axis_index("fsdp")
    c = lax.axis_index("cp")
    T = q_ref.shape[0]
    H = q_ref.shape[1] // HD
    R = F // G
    S = 2 if R % 2 == 0 else 1
    Q = F // S
    q = lax.div(f, S)
    s = lax.rem(f, S)
    twin = q * S + (S - 1 - s)
    rows = k_ref.shape[0]
    KG = F * rows
    half = T // 2
    scale = 1.0 / math.sqrt(HD)
    power = scale * math.log2(math.e)

    loads = [
        pltpu.make_async_copy(src, dst, in_sem.at[i])
        for i, (src, dst) in enumerate(
            ((k_in, k_ref), (v_in, v_ref), (q_in, q_ref), (do_in, do_ref))
        )
    ]
    stores = [
        pltpu.make_async_copy(src, dst, out_sem.at[i])
        for i, (src, dst) in enumerate(
            ((o_ref, o_out), (dq_ref, dq_out), (dk_ref, dk_out), (dv_ref, dv_out))
        )
    ]
    for load in loads:
        load.start()

    barrier = pltpu.get_barrier_semaphore()
    for d in range(1, C):
        pl.semaphore_signal(barrier, inc=1, device_id={"cp": lax.rem(c + d, C)})
    for e in range(1, Q):
        pl.semaphore_signal(barrier, inc=1, device_id={"fsdp": lax.rem(q + e, Q) * S + s})
    if S > 1:
        pl.semaphore_signal(barrier, inc=1, device_id={"fsdp": twin})

    loads[0].wait()
    loads[1].wait()
    for g in range(G):
        cp_buf[0, g, 0] = k_ref[:, g * HD : (g + 1) * HD]
        cp_buf[0, g, 1] = v_ref[:, g * HD : (g + 1) * HD]

    pl.semaphore_wait(barrier, C + Q + S - 3)

    def cp_copy(d):
        return pltpu.make_async_remote_copy(
            src_ref=cp_buf.at[0],
            dst_ref=cp_buf.at[d],
            send_sem=send1.at[d],
            recv_sem=recv1.at[d],
            device_id={"cp": lax.rem(c + d, C)},
        )

    def peer_copy(e, d):
        target = lax.rem(q + e, Q) * S + s
        return pltpu.make_async_remote_copy(
            src_ref=cp_buf.at[d, lax.div(target, R)],
            dst_ref=kv_buf.at[d, :, s, q],
            send_sem=send2.at[d],
            recv_sem=recv2.at[d],
            device_id={"fsdp": target},
        )

    def peers_all(d):
        return pltpu.make_async_remote_copy(
            src_ref=kv_buf.at[d, :, s, pl.ds(0, Q - 1)],
            dst_ref=kv_buf.at[d, :, s, pl.ds(0, Q - 1)],
            send_sem=send2.at[d],
            recv_sem=recv2.at[d],
            device_id={"fsdp": lax.rem(f + S, F)},
        )

    def twin_copy(d, source):
        return pltpu.make_async_remote_copy(
            src_ref=kv_buf.at[d, :, source],
            dst_ref=kv_buf.at[d, :, source],
            send_sem=twin_send.at[d],
            recv_sem=twin_recv.at[d],
            device_id={"fsdp": twin},
        )

    for d in range(1, C):
        cp_copy(d).start()

    def forward(d):
        for e in range(1, Q):
            peer_copy(e, d).start()
        kv_buf[d, :, s, q] = cp_buf[d, lax.div(f, R)]

    def to_twin(d):
        if Q > 1:
            peers_all(d).wait_recv()
        if S > 1:
            twin_copy(d, s).start()

    forward(0)
    loads[2].wait()
    loads[3].wait()
    for h in range(H):
        dot_buf[h] = do_ref[:, h * HD : (h + 1) * HD].astype(F32).T
        dqt_buf[h] = jnp.zeros((HD, T), F32)
        outt_buf[h] = jnp.zeros((HD, T), F32)
        peak_buf[h] = jnp.full((1, T), NEG_FILL, F32)
        total_buf[h] = jnp.zeros((1, T), F32)

    lane = lax.broadcasted_iota(jnp.int32, (1, T), 1)
    first = order_ref[2 * c] * half
    second = order_ref[2 * c + 1] * half
    row_pos = jnp.where(lane < half, first + lane, second + lane - half)

    stack = lax.broadcasted_iota(jnp.int32, (KG, 1), 0)
    owner = lax.rem(lax.div(stack, rows), Q) * S + lax.div(stack, rows * Q)
    key_base = owner * (C * rows) + lax.rem(stack, rows)

    def score_group(group):
        if S > 1:
            twin_copy(group, 1 - s).wait_recv()
        keys = rows_of(kv_buf[group, 0], KG)
        vals = rows_of(kv_buf[group, 1], KG)
        kt_buf[group] = keys.astype(F32).T.astype(BF16)
        vt = vals.astype(F32).T.astype(BF16)
        visible = key_base + lax.rem(c + C - group, C) * rows <= row_pos
        for h in range(H):
            cols = slice(h * HD, (h + 1) * HD)
            scores = jnp.where(visible, dot_nt(keys, q_ref[:, cols]), NEG_FILL)
            old = peak_buf[h]
            peak = jnp.maximum(old, jnp.max(scores, axis=0, keepdims=True))
            shrink = jnp.exp2((old - peak) * power)
            e = jnp.exp2((scores - peak) * power)
            s_buf[group, h] = e
            peak_buf[h] = peak
            seen_buf[group, h] = peak
            total_buf[h] = total_buf[h] * shrink + jnp.sum(e, axis=0, keepdims=True)
            outt_buf[h] = outt_buf[h] * shrink + dot_nn(vt, e.astype(BF16))
            dp_buf[group, h] = dot_nt(vals, do_ref[:, cols])

    def score_step(group):
        cp_copy(group + 1).wait_recv()
        forward(group + 1)
        score_group(group)
        to_twin(group + 1)

    to_twin(0)
    run_steps(0, C - 1, score_step)
    score_group(C - 1)

    for h in range(H):
        weight = 1.0 / total_buf[h]
        out = (outt_buf[h] * weight).astype(BF16).astype(F32)
        for group in range(C):
            seen_buf[group, h] = jnp.exp2((seen_buf[group, h] - peak_buf[h]) * power) * weight
        delta_buf[h] = jnp.sum(out * dot_buf[h], axis=0, keepdims=True)
        o_ref[:, h * HD : (h + 1) * HD] = out.T.astype(BF16)
    stores[0].start()

    def pair_copy(d):
        return pltpu.make_async_remote_copy(
            src_ref=send_buf.at[d, S - 1 - s],
            dst_ref=twin_buf.at[d],
            send_sem=pair_send.at[d],
            recv_sem=pair_recv.at[d],
            device_id={"fsdp": twin},
        )

    def r1_copy(e, d):
        target = lax.rem(q + e, Q)
        return pltpu.make_async_remote_copy(
            src_ref=pair_buf.at[d, target],
            dst_ref=r1_buf.at[d, q],
            send_sem=send3.at[d],
            recv_sem=recv3.at[d],
            device_id={"fsdp": target * S + s},
        )

    def r1_all(d):
        return pltpu.make_async_remote_copy(
            src_ref=pair_buf.at[d, pl.ds(0, Q - 1)],
            dst_ref=r1_buf.at[d, pl.ds(0, Q - 1)],
            send_sem=send3.at[d],
            recv_sem=recv3.at[d],
            device_id={"fsdp": lax.rem(f + S, F)},
        )

    def grad_group(group):
        key_grad = jnp.zeros((KG, HD), F32)
        value_grad = jnp.zeros((KG, HD), F32)
        for h in range(H):
            cols = slice(h * HD, (h + 1) * HD)
            prob = s_buf[group, h] * seen_buf[group, h]
            score_grad = (prob * ((dp_buf[group, h] - delta_buf[h]) * scale)).astype(BF16)
            value_grad = value_grad + dot_nn(prob.astype(BF16), do_ref[:, cols])
            key_grad = key_grad + dot_nn(score_grad, q_ref[:, cols])
            dqt_buf[h] += dot_nn(kt_buf[group], score_grad)
        send_buf[group, :, :, 0] = key_grad.reshape(S, Q, rows, HD).astype(BF16)
        send_buf[group, :, :, 1] = value_grad.reshape(S, Q, rows, HD).astype(BF16)
        if S > 1:
            pair_copy(group).start()

    def to_peers(group):
        if S > 1:
            pair_copy(group).wait_recv()
            both = send_buf[group, s].astype(F32) + twin_buf[group].astype(F32)
            pair_buf[group] = both.astype(BF16)
        else:
            pair_buf[group] = send_buf[group, s]
        for e in range(1, Q):
            r1_copy(e, group).start()
        r1_buf[group, q] = pair_buf[group, q]

    def plane_sums(group):
        if Q > 1:
            r1_all(group).wait_recv()
        parts = []
        for g in range(G):
            part = jnp.zeros((2, rows, HD), F32)
            for r in range(R // S):
                part = part + r1_buf[group, g * (R // S) + r].astype(F32)
            parts.append(part)
        return parts

    def r2_copy(d):
        return pltpu.make_async_remote_copy(
            src_ref=r2_send.at[d],
            dst_ref=r2_buf.at[d],
            send_sem=send4.at[d],
            recv_sem=recv4.at[d],
            device_id={"cp": lax.rem(c + C - d, C)},
        )

    def pass_on(group):
        for g, part in enumerate(plane_sums(group)):
            r2_send[group, g] = part.astype(BF16)
        r2_copy(group).start()

    grad_group(1 % C)

    def grad_step(group):
        grad_group(lax.rem(group + 1, C))
        to_peers(group)

    def grad_pass(group):
        grad_step(group)
        pass_on(group - 1)

    if C > 1:
        grad_step(1)
    run_steps(2, C, grad_pass)
    to_peers(0)
    if C > 1:
        pass_on(C - 1)
    for h in range(H):
        dq_ref[:, h * HD : (h + 1) * HD] = dqt_buf[h].T.astype(BF16)
    stores[1].start()
    own_sums = plane_sums(0)
    for d in range(1, C):
        r2_copy(d).wait_recv()
    for g in range(G):
        whole = own_sums[g]
        for d in range(1, C):
            whole = whole + r2_buf[d, g].astype(F32)
        dk_ref[:, g * HD : (g + 1) * HD] = whole[0]
        dv_ref[:, g * HD : (g + 1) * HD] = whole[1]

    stores[2].start()
    stores[3].start()

    for d in range(1, C):
        cp_copy(d).wait_send()
        r2_copy(d).wait_send()
    for d in range(C):
        if Q > 1:
            peers_all(d).wait_send()
            r1_all(d).wait_send()
        if S > 1:
            twin_copy(d, s).wait_send()
            pair_copy(d).wait_send()
    for store in stores:
        store.wait()


def hand_over(*refs):
    count = (len(refs) - 2) // 3
    sems = refs[-2:]
    loads = [
        pltpu.make_async_copy(refs[i], refs[2 * count + i], sems[0].at[i]) for i in range(count)
    ]
    stores = [
        pltpu.make_async_copy(refs[2 * count + i], refs[count + i], sems[1].at[i])
        for i in range(count)
    ]
    for load in loads:
        load.start()
    for load, store in zip(loads, stores):
        load.wait()
        store.start()
    for store in stores:
        store.wait()


def per_device(queries, key_vectors, value_vectors, out_grads, pair_order):
    C = lax.axis_size("cp")
    F = lax.axis_size("fsdp")
    T, width = queries.shape
    H = width // HD
    rows, kv_width = key_vectors.shape
    G = kv_width // HD
    KG = F * rows
    S = 2 if (F // G) % 2 == 0 else 1
    Q = F // S
    whole = pl.BlockSpec(memory_space=pl.ANY)
    dma = pltpu.SemaphoreType.DMA
    shapes = (
        jax.ShapeDtypeStruct((T, width), BF16),
        jax.ShapeDtypeStruct((T, width), BF16),
        jax.ShapeDtypeStruct((rows, kv_width), F32),
        jax.ShapeDtypeStruct((rows, kv_width), F32),
    )
    results = pl.pallas_call(
        functools.partial(kernel, F, C, G),
        out_shape=shapes,
        in_specs=[pl.BlockSpec(memory_space=pltpu.SMEM)] + [whole] * 4,
        out_specs=(whole,) * 4,
        scratch_shapes=[
            pltpu.VMEM((T, width), BF16),
            pltpu.VMEM((rows, kv_width), BF16),
            pltpu.VMEM((rows, kv_width), BF16),
            pltpu.VMEM((T, width), BF16),
            pltpu.VMEM((T, width), BF16),
            pltpu.VMEM((T, width), BF16),
            pltpu.VMEM((rows, kv_width), F32),
            pltpu.VMEM((rows, kv_width), F32),
            dma((4,)),
            dma((4,)),
            pltpu.VMEM((C, G, 2, rows, HD), BF16),
            pltpu.VMEM((C, 2, S, Q, rows, HD), BF16),
            pltpu.VMEM((C, S, Q, 2, rows, HD), BF16),
            pltpu.VMEM((C, Q, 2, rows, HD), BF16),
            pltpu.VMEM((C, Q, 2, rows, HD), BF16),
            pltpu.VMEM((C, Q, 2, rows, HD), BF16),
            pltpu.VMEM((C, G, 2, rows, HD), BF16),
            pltpu.VMEM((C, G, 2, rows, HD), BF16),
            pltpu.VMEM((C, HD, KG), BF16),
            pltpu.VMEM((H, HD, T), F32),
            pltpu.VMEM((C, H, KG, T), F32),
            pltpu.VMEM((C, H, KG, T), F32),
            pltpu.VMEM((H, 1, T), F32),
            pltpu.VMEM((H, 1, T), F32),
            pltpu.VMEM((H, HD, T), F32),
            pltpu.VMEM((C, H, 1, T), F32),
            pltpu.VMEM((H, 1, T), F32),
            pltpu.VMEM((H, HD, T), F32),
        ]
        + [dma((C,))] * 12,
        compiler_params=pltpu.CompilerParams(
            collective_id=0, has_side_effects=True, vmem_limit_bytes=56 * 1024 * 1024
        ),
    )(pair_order, queries, key_vectors, value_vectors, out_grads)
    return pl.pallas_call(
        hand_over,
        out_shape=shapes,
        in_specs=[whole] * 4,
        out_specs=(whole,) * 4,
        scratch_shapes=[pltpu.VMEM(a.shape, a.dtype) for a in shapes] + [dma((4,))] * 2,
        compiler_params=pltpu.CompilerParams(vmem_limit_bytes=56 * 1024 * 1024),
    )(*results)


def solution(mesh):
    return jax.shard_map(
        per_device,
        mesh=mesh,
        in_specs=(
            P("cp", "fsdp"),
            P(("fsdp", "cp"), None),
            P(("fsdp", "cp"), None),
            P("cp", "fsdp"),
            P(),
        ),
        out_specs=(
            P("cp", "fsdp"),
            P("cp", "fsdp"),
            P(("fsdp", "cp"), None),
            P(("fsdp", "cp"), None),
        ),
        check_vma=False,
    )
```

profile of v0, /device:TPU:0, one launch (start us, length us, event | category | flops | bytes accessed | tf_op | source)
XLA Modules:
  0.0 37.7 jit_solution(10776537334867139486)
XLA Ops:
  0.6 35.2 %shard_map.84 = (bf16[256,512]{1,0:T(8,128)(2,1)}, bf16[256,512]{1,0:T(8,128)(2,1)}, f32[32,256]{1,0:T(8,128)}, f32[32,256]{1,0:T(8,128)}) custom-call(s32[8]{0:T(128)} %order_ref.1, bf16[256,512]{1,0:T(8,128)(2,1)} %q_in.1, bf16[32,256]{1,0:T(8,128)(2,1)} %k_in.1, bf16[32,256]{1,0:T(8,128)(2,1)} %v_in.1, bf16[256,512]{1,0:T(8,128)(2,1)} %do_in.1), custom_call_target="tpu_custom_call" | custom-call | tf_op jit(solution)/shard_map/pallas_call | solution.py:413
  35.9 1.8 %shard_map.85 = (bf16[256,512]{1,0:T(8,128)(2,1)}, bf16[256,512]{1,0:T(8,128)(2,1)}, f32[32,256]{1,0:T(8,128)}, f32[32,256]{1,0:T(8,128)}) custom-call(bf16[256,512]{1,0:T(8,128)(2,1)} %get-tuple-element.8.refs_0_, bf16[256,512]{1,0:T(8,128)(2,1)} %get-tuple-element.9.refs_1_, f32[32,256]{1,0:T(8,128)} %get-tuple-element.10.refs_2_, ...), custom_call_target="tpu_custom_call" | custom-call | tf_op jit(solution)/shard_map/pallas_call | solution.py:453
where the time goes:
time: 38 us; the launch traced here: 37.7 us
  Pallas kernels  37.1 us (98%)
  between operations  0.64 us (2%)
    pallas_call x1, Pallas kernels, per_device(): pl.pallas_call(functools.partial(kernel, F, C, G), out_shape=shapes, in_s...  35.2 us
    pallas_call x1, Pallas kernels, per_device(): pl.pallas_call(hand_over, out_shape=shapes, in_specs=[whole] * 4, out_spe...  1.82 us

commit v1 on v0

--- a/solution.py
+++ b/solution.py
@@ -12,6 +12,7 @@
 NEG_FILL = -1e30
 F32 = jnp.float32
 BF16 = jnp.bfloat16
+STRIP = 64
 
 
 def rows_of(blocks, count):
@@ -34,6 +35,15 @@
             step(i)
     else:
         lax.fori_loop(low, high, lambda i, carry: (step(i), carry)[1], 0)
+
+
+def loop_steps(low, high, step):
+    lax.fori_loop(low, high, lambda i, carry: (step(i), carry)[1], 0)
+
+
+def fold_rows(fn, tile):
+    rows, lanes = tile.shape
+    return fn(tile.reshape(rows // 8, 8, lanes), axis=0)
 
 
 def kernel(
@@ -68,7 +78,11 @@
     r2_send,
     r2_buf,
     kt_buf,
-    dot_buf,
+    vt_buf,
+    key_base,
+    p_buf,
+    prob_buf,
+    grad_buf,
     s_buf,
     dp_buf,
     peak_buf,
@@ -92,8 +106,7 @@
 ):
     f = lax.axis_index("fsdp")
     c = lax.axis_index("cp")
-    T = q_ref.shape[0]
-    H = q_ref.shape[1] // HD
+    H, T, _ = q_ref.shape
     R = F // G
     S = 2 if R % 2 == 0 else 1
     Q = F // S
@@ -106,18 +119,15 @@
     scale = 1.0 / math.sqrt(HD)
     power = scale * math.log2(math.e)
 
-    loads = [
-        pltpu.make_async_copy(src, dst, in_sem.at[i])
-        for i, (src, dst) in enumerate(
-            ((k_in, k_ref), (v_in, v_ref), (q_in, q_ref), (do_in, do_ref))
-        )
-    ]
-    stores = [
-        pltpu.make_async_copy(src, dst, out_sem.at[i])
-        for i, (src, dst) in enumerate(
-            ((o_ref, o_out), (dq_ref, dq_out), (dk_ref, dk_out), (dv_ref, dv_out))
-        )
-    ]
+    cut = [pl.ds(h * HD, HD) for h in range(H)]
+    moves = [(k_in, k_ref), (v_in, v_ref)]
+    moves += [(q_in.at[:, cut[h]], q_ref.at[h]) for h in range(H)]
+    moves += [(do_in.at[:, cut[h]], do_ref.at[h]) for h in range(H)]
+    loads = [pltpu.make_async_copy(a, b, in_sem.at[i]) for i, (a, b) in enumerate(moves)]
+    moves = [(dk_ref, dk_out), (dv_ref, dv_out)]
+    moves += [(o_ref.at[h], o_out.at[:, cut[h]]) for h in range(H)]
+    moves += [(dq_ref.at[h], dq_out.at[:, cut[h]]) for h in range(H)]
+    stores = [pltpu.make_async_copy(a, b, out_sem.at[i]) for i, (a, b) in enumerate(moves)]
     for load in loads:
         load.start()
 
@@ -189,64 +199,82 @@
             twin_copy(d, s).start()
 
     forward(0)
-    loads[2].wait()
-    loads[3].wait()
     for h in range(H):
-        dot_buf[h] = do_ref[:, h * HD : (h + 1) * HD].astype(F32).T
         dqt_buf[h] = jnp.zeros((HD, T), F32)
         outt_buf[h] = jnp.zeros((HD, T), F32)
         peak_buf[h] = jnp.full((1, T), NEG_FILL, F32)
         total_buf[h] = jnp.zeros((1, T), F32)
-
+        delta_buf[h] = jnp.zeros((1, T), F32)
     lane = lax.broadcasted_iota(jnp.int32, (1, T), 1)
     first = order_ref[2 * c] * half
     second = order_ref[2 * c + 1] * half
     row_pos = jnp.where(lane < half, first + lane, second + lane - half)
-
-    stack = lax.broadcasted_iota(jnp.int32, (KG, 1), 0)
+    stack = lax.broadcasted_iota(jnp.int32, (KG, HD), 0)
     owner = lax.rem(lax.div(stack, rows), Q) * S + lax.div(stack, rows * Q)
-    key_base = owner * (C * rows) + lax.rem(stack, rows)
+    key_base[...] = owner * (C * rows) + lax.rem(stack, rows)
+    for load in loads[2:]:
+        load.wait()
+
+    def relay(d):
+        cp_copy(d).wait_recv()
+        forward(d)
+
+    run_steps(1, C, relay)
+    to_twin(0)
+    strips = [slice(k, min(k + STRIP, KG)) for k in range(0, KG, STRIP)]
 
     def score_group(group):
+        @pl.when(group < C - 1)
+        def _():
+            to_twin(group + 1)
+
         if S > 1:
             twin_copy(group, 1 - s).wait_recv()
         keys = rows_of(kv_buf[group, 0], KG)
         vals = rows_of(kv_buf[group, 1], KG)
-        kt_buf[group] = keys.astype(F32).T.astype(BF16)
-        vt = vals.astype(F32).T.astype(BF16)
-        visible = key_base + lax.rem(c + C - group, C) * rows <= row_pos
+        kt_buf[group] = keys.T
+        vt_buf[...] = vals.T
+        limit = row_pos - lax.rem(c + C - group, C) * rows
+
+        def visible(strip):
+            return jnp.concatenate([key_base[strip]] * (T // HD), axis=1) <= limit
+
         for h in range(H):
-            cols = slice(h * HD, (h + 1) * HD)
-            scores = jnp.where(visible, dot_nt(keys, q_ref[:, cols]), NEG_FILL)
+            s_buf[group, h] = dot_nt(keys, q_ref[h])
+            dp_buf[group, h] = dot_nt(vals, do_ref[h])
+        for h in range(H):
+            peak8 = jnp.full((8, T), NEG_FILL, F32)
+            for strip in strips:
+                scores = jnp.where(visible(strip), s_buf[group, h, strip], NEG_FILL)
+                peak8 = jnp.maximum(peak8, fold_rows(jnp.max, scores))
             old = peak_buf[h]
-            peak = jnp.maximum(old, jnp.max(scores, axis=0, keepdims=True))
+            peak = jnp.maximum(old, jnp.max(peak8, axis=0, keepdims=True))
             shrink = jnp.exp2((old - peak) * power)
-            e = jnp.exp2((scores - peak) * power)
-            s_buf[group, h] = e
+            total8 = jnp.zeros((8, T), F32)
+            delta8 = jnp.zeros((8, T), F32)
+            for strip in strips:
+                e = jnp.exp2((s_buf[group, h, strip] - peak) * power)
+                e = jnp.where(visible(strip), e, 0.0)
+                s_buf[group, h, strip] = e
+                p_buf[h, strip] = e.astype(BF16)
+                total8 = total8 + fold_rows(jnp.sum, e)
+                delta8 = delta8 + fold_rows(jnp.sum, e * dp_buf[group, h, strip])
             peak_buf[h] = peak
             seen_buf[group, h] = peak
-            total_buf[h] = total_buf[h] * shrink + jnp.sum(e, axis=0, keepdims=True)
-            outt_buf[h] = outt_buf[h] * shrink + dot_nn(vt, e.astype(BF16))
-            dp_buf[group, h] = dot_nt(vals, do_ref[:, cols])
-
-    def score_step(group):
-        cp_copy(group + 1).wait_recv()
-        forward(group + 1)
-        score_group(group)
-        to_twin(group + 1)
-
-    to_twin(0)
-    run_steps(0, C - 1, score_step)
-    score_group(C - 1)
+            total_buf[h] = total_buf[h] * shrink + jnp.sum(total8, axis=0, keepdims=True)
+            delta_buf[h] = delta_buf[h] * shrink + jnp.sum(delta8, axis=0, keepdims=True)
+            outt_buf[h] = outt_buf[h] * shrink + dot_nn(vt_buf[...], p_buf[h])
+
+    loop_steps(0, C, score_group)
 
     for h in range(H):
         weight = 1.0 / total_buf[h]
-        out = (outt_buf[h] * weight).astype(BF16).astype(F32)
         for group in range(C):
             seen_buf[group, h] = jnp.exp2((seen_buf[group, h] - peak_buf[h]) * power) * weight
-        delta_buf[h] = jnp.sum(out * dot_buf[h], axis=0, keepdims=True)
-        o_ref[:, h * HD : (h + 1) * HD] = out.T.astype(BF16)
-    stores[0].start()
+        delta_buf[h] = delta_buf[h] * weight
+        o_ref[h] = (outt_buf[h] * weight).astype(BF16).T
+    for store in stores[2 : 2 + H]:
+        store.start()
 
     def pair_copy(d):
         return pltpu.make_async_remote_copy(
@@ -277,15 +305,18 @@
         )
 
     def grad_group(group):
-        key_grad = jnp.zeros((KG, HD), F32)
-        value_grad = jnp.zeros((KG, HD), F32)
         for h in range(H):
-            cols = slice(h * HD, (h + 1) * HD)
-            prob = s_buf[group, h] * seen_buf[group, h]
-            score_grad = (prob * ((dp_buf[group, h] - delta_buf[h]) * scale)).astype(BF16)
-            value_grad = value_grad + dot_nn(prob.astype(BF16), do_ref[:, cols])
-            key_grad = key_grad + dot_nn(score_grad, q_ref[:, cols])
-            dqt_buf[h] += dot_nn(kt_buf[group], score_grad)
+            cols = slice(h * T, (h + 1) * T)
+            weight = seen_buf[group, h]
+            scaled = weight * scale
+            for strip in strips:
+                e = s_buf[group, h, strip]
+                grad = (e * scaled) * (dp_buf[group, h, strip] - delta_buf[h])
+                prob_buf[strip, cols] = (e * weight).astype(BF16)
+                grad_buf[strip, cols] = grad.astype(BF16)
+            dqt_buf[h] += dot_nn(kt_buf[group], grad_buf[:, cols])
+        value_grad = dot_nn(prob_buf[...], do_ref[...].reshape(H * T, HD))
+        key_grad = dot_nn(grad_buf[...], q_ref[...].reshape(H * T, HD))
         send_buf[group, :, :, 0] = key_grad.reshape(S, Q, rows, HD).astype(BF16)
         send_buf[group, :, :, 1] = value_grad.reshape(S, Q, rows, HD).astype(BF16)
         if S > 1:
@@ -327,25 +358,25 @@
             r2_send[group, g] = part.astype(BF16)
         r2_copy(group).start()
 
-    grad_group(1 % C)
-
-    def grad_step(group):
-        grad_group(lax.rem(group + 1, C))
-        to_peers(group)
-
-    def grad_pass(group):
-        grad_step(group)
-        pass_on(group - 1)
-
-    if C > 1:
-        grad_step(1)
-    run_steps(2, C, grad_pass)
+    def grad_step(step):
+        grad_group(lax.rem(step + 1, C))
+
+        @pl.when(step >= 1)
+        def _():
+            to_peers(step)
+
+        @pl.when(step >= 2)
+        def _():
+            pass_on(step - 1)
+
+    loop_steps(0, C, grad_step)
     to_peers(0)
     if C > 1:
         pass_on(C - 1)
     for h in range(H):
-        dq_ref[:, h * HD : (h + 1) * HD] = dqt_buf[h].T.astype(BF16)
-    stores[1].start()
+        dq_ref[h] = dqt_buf[h].astype(BF16).T
+    for store in stores[2 + H :]:
+        store.start()
     own_sums = plane_sums(0)
     for d in range(1, C):
         r2_copy(d).wait_recv()
@@ -356,8 +387,8 @@
         dk_ref[:, g * HD : (g + 1) * HD] = whole[0]
         dv_ref[:, g * HD : (g + 1) * HD] = whole[1]
 
-    stores[2].start()
-    stores[3].start()
+    stores[0].start()
+    stores[1].start()
 
     for d in range(1, C):
         cp_copy(d).wait_send()
@@ -416,16 +447,16 @@
         in_specs=[pl.BlockSpec(memory_space=pltpu.SMEM)] + [whole] * 4,
         out_specs=(whole,) * 4,
         scratch_shapes=[
-            pltpu.VMEM((T, width), BF16),
+            pltpu.VMEM((H, T, HD), BF16),
             pltpu.VMEM((rows, kv_width), BF16),
             pltpu.VMEM((rows, kv_width), BF16),
-            pltpu.VMEM((T, width), BF16),
-            pltpu.VMEM((T, width), BF16),
-            pltpu.VMEM((T, width), BF16),
+            pltpu.VMEM((H, T, HD), BF16),
+            pltpu.VMEM((H, T, HD), BF16),
+            pltpu.VMEM((H, T, HD), BF16),
             pltpu.VMEM((rows, kv_width), F32),
             pltpu.VMEM((rows, kv_width), F32),
-            dma((4,)),
-            dma((4,)),
+            dma((2 + 2 * H,)),
+            dma((2 + 2 * H,)),
             pltpu.VMEM((C, G, 2, rows, HD), BF16),
             pltpu.VMEM((C, 2, S, Q, rows, HD), BF16),
             pltpu.VMEM((C, S, Q, 2, rows, HD), BF16),
@@ -435,7 +466,11 @@
             pltpu.VMEM((C, G, 2, rows, HD), BF16),
             pltpu.VMEM((C, G, 2, rows, HD), BF16),
             pltpu.VMEM((C, HD, KG), BF16),
-            pltpu.VMEM((H, HD, T), F32),
+            pltpu.VMEM((HD, KG), BF16),
+            pltpu.VMEM((KG, HD), jnp.int32),
+            pltpu.VMEM((H, KG, T), BF16),
+            pltpu.VMEM((KG, H * T), BF16),
+            pltpu.VMEM((KG, H * T), BF16),
             pltpu.VMEM((C, H, KG, T), F32),
             pltpu.VMEM((C, H, KG, T), F32),
             pltpu.VMEM((H, 1, T), F32),

time: 38 us -> 34.3 us (0.903)
  Pallas kernels: 37.1 us -> 33.4 us
    pallas_call x1, Pallas kernels: 35.2 us -> 31.6 us  [per_device(): pl.pallas_call(functools.partial(kernel, F, C, G), out_shape=shapes, in_s...]
where the time goes in v1:
time: 34.3 us; the launch traced here: 34 us
  Pallas kernels  33.4 us (97%)
  between operations  0.64 us (2%)
    pallas_call x1, Pallas kernels, per_device(): pl.pallas_call(functools.partial(kernel, F, C, G), out_shape=shapes, in_s...  31.6 us
    pallas_call x1, Pallas kernels, per_device(): pl.pallas_call(hand_over, out_shape=shapes, in_specs=[whole] * 4, out_spe...  1.82 us

profile of v1, /device:TPU:0, one launch (start us, length us, event | category | flops | bytes accessed | tf_op | source)
XLA Modules:
  0.0 34.0 jit_solution(11962358995348532985)
XLA Ops:
  0.6 31.6 %shard_map.84 = (bf16[256,512]{1,0:T(8,128)(2,1)}, bf16[256,512]{1,0:T(8,128)(2,1)}, f32[32,256]{1,0:T(8,128)}, f32[32,256]{1,0:T(8,128)}) custom-call(s32[8]{0:T(128)} %order_ref.1, bf16[256,512]{1,0:T(8,128)(2,1)} %q_in.1, bf16[32,256]{1,0:T(8,128)(2,1)} %k_in.1, bf16[32,256]{1,0:T(8,128)(2,1)} %v_in.1, bf16[256,512]{1,0:T(8,128)(2,1)} %do_in.1), custom_call_target="tpu_custom_call" | custom-call | tf_op jit(solution)/shard_map/pallas_call | solution.py:444
  32.2 1.8 %shard_map.85 = (bf16[256,512]{1,0:T(8,128)(2,1)}, bf16[256,512]{1,0:T(8,128)(2,1)}, f32[32,256]{1,0:T(8,128)}, f32[32,256]{1,0:T(8,128)}) custom-call(bf16[256,512]{1,0:T(8,128)(2,1)} %get-tuple-element.8.refs_0_, bf16[256,512]{1,0:T(8,128)(2,1)} %get-tuple-element.9.refs_1_, f32[32,256]{1,0:T(8,128)} %get-tuple-element.10.refs_2_, ...), custom_call_target="tpu_custom_call" | custom-call | tf_op jit(solution)/shard_map/pallas_call | solution.py:488

commit v2 on v1

--- a/solution.py
+++ b/solution.py
@@ -63,12 +63,7 @@
     k_ref,
     v_ref,
     do_ref,
-    o_ref,
-    dq_ref,
-    dk_ref,
-    dv_ref,
     in_sem,
-    out_sem,
     cp_buf,
     kv_buf,
     send_buf,
@@ -119,15 +114,11 @@
     scale = 1.0 / math.sqrt(HD)
     power = scale * math.log2(math.e)
 
-    cut = [pl.ds(h * HD, HD) for h in range(H)]
+    cut = [slice(h * HD, (h + 1) * HD) for h in range(H)]
     moves = [(k_in, k_ref), (v_in, v_ref)]
     moves += [(q_in.at[:, cut[h]], q_ref.at[h]) for h in range(H)]
     moves += [(do_in.at[:, cut[h]], do_ref.at[h]) for h in range(H)]
     loads = [pltpu.make_async_copy(a, b, in_sem.at[i]) for i, (a, b) in enumerate(moves)]
-    moves = [(dk_ref, dk_out), (dv_ref, dv_out)]
-    moves += [(o_ref.at[h], o_out.at[:, cut[h]]) for h in range(H)]
-    moves += [(dq_ref.at[h], dq_out.at[:, cut[h]]) for h in range(H)]
-    stores = [pltpu.make_async_copy(a, b, out_sem.at[i]) for i, (a, b) in enumerate(moves)]
     for load in loads:
         load.start()
 
@@ -208,7 +199,14 @@
     lane = lax.broadcasted_iota(jnp.int32, (1, T), 1)
     first = order_ref[2 * c] * half
     second = order_ref[2 * c + 1] * half
-    row_pos = jnp.where(lane < half, first + lane, second + lane - half)
+    low, high = jnp.minimum(first, second), jnp.maximum(first, second)
+    row_pos = jnp.where(lane < half, low + lane, high + lane - half)
+    swapped = jnp.full((8, HD), first, jnp.int32) > jnp.full((8, HD), second, jnp.int32)
+
+    def in_order(a, b):
+        flip = jnp.tile(swapped, (a.shape[0] // 8, a.shape[1] // HD))
+        return jnp.where(flip, b, a), jnp.where(flip, a, b)
+
     stack = lax.broadcasted_iota(jnp.int32, (KG, HD), 0)
     owner = lax.rem(lax.div(stack, rows), Q) * S + lax.div(stack, rows * Q)
     key_base[...] = owner * (C * rows) + lax.rem(stack, rows)
@@ -219,9 +217,27 @@
         cp_copy(d).wait_recv()
         forward(d)
 
+    for ref in (q_ref, do_ref):
+        for h in range(H):
+            a, b = in_order(ref[h, :half].astype(F32), ref[h, half:].astype(F32))
+            ref[h, :half] = a.astype(BF16)
+            ref[h, half:] = b.astype(BF16)
     run_steps(1, C, relay)
     to_twin(0)
-    strips = [slice(k, min(k + STRIP, KG)) for k in range(0, KG, STRIP)]
+    reach = KG // S // 2 if Q % 2 == 0 else KG
+    strip_rows = min(STRIP, reach)
+    spans = (slice(0, half), slice(half, T))
+    strips = []
+    for k in range(0, KG, strip_rows):
+        parts = (0, 1) if (k // reach) % 2 == 0 else (1,)
+        strips.append((slice(k, k + strip_rows), parts))
+        if len(parts) == 1:
+            empty = slice(k, k + strip_rows)
+            for h in range(H):
+                p_buf[h, empty, :half] = jnp.zeros((strip_rows, half), BF16)
+                cols = slice(h * T, h * T + half)
+                prob_buf[empty, cols] = jnp.zeros((strip_rows, half), BF16)
+                grad_buf[empty, cols] = jnp.zeros((strip_rows, half), BF16)
 
     def score_group(group):
         @pl.when(group < C - 1)
@@ -236,29 +252,37 @@
         vt_buf[...] = vals.T
         limit = row_pos - lax.rem(c + C - group, C) * rows
 
-        def visible(strip):
-            return jnp.concatenate([key_base[strip]] * (T // HD), axis=1) <= limit
+        def visible(strip, span):
+            return jnp.concatenate([key_base[strip]] * (half // HD), axis=1) <= limit[:, span]
 
         for h in range(H):
             s_buf[group, h] = dot_nt(keys, q_ref[h])
             dp_buf[group, h] = dot_nt(vals, do_ref[h])
         for h in range(H):
-            peak8 = jnp.full((8, T), NEG_FILL, F32)
-            for strip in strips:
-                scores = jnp.where(visible(strip), s_buf[group, h, strip], NEG_FILL)
-                peak8 = jnp.maximum(peak8, fold_rows(jnp.max, scores))
+            peak8 = [jnp.full((8, half), NEG_FILL, F32)] * 2
+            for strip, parts in strips:
+                for part in parts:
+                    span = spans[part]
+                    scores = jnp.where(visible(strip, span), s_buf[group, h, strip, span], NEG_FILL)
+                    peak8[part] = jnp.maximum(peak8[part], fold_rows(jnp.max, scores))
             old = peak_buf[h]
+            peak8 = jnp.concatenate(peak8, axis=1)
             peak = jnp.maximum(old, jnp.max(peak8, axis=0, keepdims=True))
             shrink = jnp.exp2((old - peak) * power)
-            total8 = jnp.zeros((8, T), F32)
-            delta8 = jnp.zeros((8, T), F32)
-            for strip in strips:
-                e = jnp.exp2((s_buf[group, h, strip] - peak) * power)
-                e = jnp.where(visible(strip), e, 0.0)
-                s_buf[group, h, strip] = e
-                p_buf[h, strip] = e.astype(BF16)
-                total8 = total8 + fold_rows(jnp.sum, e)
-                delta8 = delta8 + fold_rows(jnp.sum, e * dp_buf[group, h, strip])
+            total8 = [jnp.zeros((8, half), F32)] * 2
+            delta8 = [jnp.zeros((8, half), F32)] * 2
+            for strip, parts in strips:
+                for part in parts:
+                    span = spans[part]
+                    e = jnp.exp2((s_buf[group, h, strip, span] - peak[:, span]) * power)
+                    e = jnp.where(visible(strip, span), e, 0.0)
+                    s_buf[group, h, strip, span] = e
+                    p_buf[h, strip, span] = e.astype(BF16)
+                    total8[part] = total8[part] + fold_rows(jnp.sum, e)
+                    moved = e * dp_buf[group, h, strip, span]
+                    delta8[part] = delta8[part] + fold_rows(jnp.sum, moved)
+            total8 = jnp.concatenate(total8, axis=1)
+            delta8 = jnp.concatenate(delta8, axis=1)
             peak_buf[h] = peak
             seen_buf[group, h] = peak
             total_buf[h] = total_buf[h] * shrink + jnp.sum(total8, axis=0, keepdims=True)
@@ -267,14 +291,17 @@
 
     loop_steps(0, C, score_group)
 
+    def put_rows(ref, h, columns):
+        a, b = in_order(columns[:, :half], columns[:, half:])
+        ref[:half, cut[h]] = a.astype(BF16).T
+        ref[half:, cut[h]] = b.astype(BF16).T
+
     for h in range(H):
         weight = 1.0 / total_buf[h]
         for group in range(C):
             seen_buf[group, h] = jnp.exp2((seen_buf[group, h] - peak_buf[h]) * power) * weight
         delta_buf[h] = delta_buf[h] * weight
-        o_ref[h] = (outt_buf[h] * weight).astype(BF16).T
-    for store in stores[2 : 2 + H]:
-        store.start()
+        put_rows(o_out, h, outt_buf[h] * weight)
 
     def pair_copy(d):
         return pltpu.make_async_remote_copy(
@@ -309,11 +336,15 @@
             cols = slice(h * T, (h + 1) * T)
             weight = seen_buf[group, h]
             scaled = weight * scale
-            for strip in strips:
-                e = s_buf[group, h, strip]
-                grad = (e * scaled) * (dp_buf[group, h, strip] - delta_buf[h])
-                prob_buf[strip, cols] = (e * weight).astype(BF16)
-                grad_buf[strip, cols] = grad.astype(BF16)
+            delta = delta_buf[h]
+            for strip, parts in strips:
+                for part in parts:
+                    span = spans[part]
+                    put = slice(h * T + span.start, h * T + span.stop)
+                    e = s_buf[group, h, strip, span]
+                    apart = dp_buf[group, h, strip, span] - delta[:, span]
+                    prob_buf[strip, put] = (e * weight[:, span]).astype(BF16)
+                    grad_buf[strip, put] = ((e * scaled[:, span]) * apart).astype(BF16)
             dqt_buf[h] += dot_nn(kt_buf[group], grad_buf[:, cols])
         value_grad = dot_nn(prob_buf[...], do_ref[...].reshape(H * T, HD))
         key_grad = dot_nn(grad_buf[...], q_ref[...].reshape(H * T, HD))
@@ -374,9 +405,7 @@
     if C > 1:
         pass_on(C - 1)
     for h in range(H):
-        dq_ref[h] = dqt_buf[h].astype(BF16).T
-    for store in stores[2 + H :]:
-        store.start()
+        put_rows(dq_out, h, dqt_buf[h])
     own_sums = plane_sums(0)
     for d in range(1, C):
         r2_copy(d).wait_recv()
@@ -384,11 +413,9 @@
         whole = own_sums[g]
         for d in range(1, C):
             whole = whole + r2_buf[d, g].astype(F32)
-        dk_ref[:, g * HD : (g + 1) * HD] = whole[0]
-        dv_ref[:, g * HD : (g + 1) * HD] = whole[1]
-
-    stores[0].start()
-    stores[1].start()
+        dk_out[:, g * HD : (g + 1) * HD] = whole[0]
+        dv_out[:, g * HD : (g + 1) * HD] = whole[1]
+
 
     for d in range(1, C):
         cp_copy(d).wait_send()
@@ -400,24 +427,15 @@
         if S > 1:
             twin_copy(d, s).wait_send()
             pair_copy(d).wait_send()
+
+
+def hand_over(*refs):
+    count = len(refs) // 2
+    sems = refs[-1]
+    stores = [
+        pltpu.make_async_copy(refs[i], refs[count + i], sems.at[i]) for i in range(count)
+    ]
     for store in stores:
-        store.wait()
-
-
-def hand_over(*refs):
-    count = (len(refs) - 2) // 3
-    sems = refs[-2:]
-    loads = [
-        pltpu.make_async_copy(refs[i], refs[2 * count + i], sems[0].at[i]) for i in range(count)
-    ]
-    stores = [
-        pltpu.make_async_copy(refs[2 * count + i], refs[count + i], sems[1].at[i])
-        for i in range(count)
-    ]
-    for load in loads:
-        load.start()
-    for load, store in zip(loads, stores):
-        load.wait()
         store.start()
     for store in stores:
         store.wait()
@@ -434,6 +452,7 @@
     S = 2 if (F // G) % 2 == 0 else 1
     Q = F // S
     whole = pl.BlockSpec(memory_space=pl.ANY)
+    local = pl.BlockSpec(memory_space=pltpu.VMEM)
     dma = pltpu.SemaphoreType.DMA
     shapes = (
         jax.ShapeDtypeStruct((T, width), BF16),
@@ -443,19 +462,14 @@
     )
     results = pl.pallas_call(
         functools.partial(kernel, F, C, G),
-        out_shape=shapes,
+        out_shape=tuple(pltpu.VMEM(a.shape, a.dtype) for a in shapes),
         in_specs=[pl.BlockSpec(memory_space=pltpu.SMEM)] + [whole] * 4,
-        out_specs=(whole,) * 4,
+        out_specs=(local,) * 4,
         scratch_shapes=[
             pltpu.VMEM((H, T, HD), BF16),
             pltpu.VMEM((rows, kv_width), BF16),
             pltpu.VMEM((rows, kv_width), BF16),
             pltpu.VMEM((H, T, HD), BF16),
-            pltpu.VMEM((H, T, HD), BF16),
-            pltpu.VMEM((H, T, HD), BF16),
-            pltpu.VMEM((rows, kv_width), F32),
-            pltpu.VMEM((rows, kv_width), F32),
-            dma((2 + 2 * H,)),
             dma((2 + 2 * H,)),
             pltpu.VMEM((C, G, 2, rows, HD), BF16),
             pltpu.VMEM((C, 2, S, Q, rows, HD), BF16),
@@ -488,11 +502,11 @@
     return pl.pallas_call(
         hand_over,
         out_shape=shapes,
-        in_specs=[whole] * 4,
+        in_specs=[local] * 4,
         out_specs=(whole,) * 4,
-        scratch_shapes=[pltpu.VMEM(a.shape, a.dtype) for a in shapes] + [dma((4,))] * 2,
+        scratch_shapes=[dma((4,))],
         compiler_params=pltpu.CompilerParams(vmem_limit_bytes=56 * 1024 * 1024),
-    )(*results)
+    )(*[pltpu.with_memory_space_constraint(a, pltpu.VMEM) for a in results])
 
 
 def solution(mesh):

time: 34.3 us -> 32.6 us (0.950)
  Pallas kernels: 33.4 us -> 31.7 us
    pallas_call x2, Pallas kernels: 33.4 us -> 31.7 us  [the longest x1 30.9 us: per_device(): pl.pallas_call(functools.partial(kernel, F, C, G), out_shape=tuple((pltpu...]
where the time goes in v2:
time: 32.6 us; the launch traced here: 32.3 us
  Pallas kernels  31.7 us (97%)
  between operations  0.64 us (2%)
    pallas_call x1, Pallas kernels, per_device(): pl.pallas_call(functools.partial(kernel, F, C, G), out_shape=tuple((pltpu...  30.9 us
    pallas_call x1, Pallas kernels, per_device(): pl.pallas_call(hand_over, out_shape=shapes, in_specs=[local] * 4, out_spe...  0.84 us

profile of v2, /device:TPU:0, one launch (start us, length us, event | category | flops | bytes accessed | tf_op | source)
XLA Modules:
  0.0 32.3 jit_solution(9641122659182242201)
XLA Ops:
  0.6 30.9 %shard_map.84 = (bf16[256,512]{1,0:T(8,128)(2,1)S(1)}, bf16[256,512]{1,0:T(8,128)(2,1)S(1)}, f32[32,256]{1,0:T(8,128)S(1)}, f32[32,256]{1,0:T(8,128)S(1)}) custom-call(s32[8]{0:T(128)} %order_ref.1, bf16[256,512]{1,0:T(8,128)(2,1)} %q_in.1, bf16[32,256]{1,0:T(8,128)(2,1)} %k_in.1, bf16[32,256]{1,0:T(8,128)(2,1)} %v_in.1, bf16[256,512]{1,0:T(8,128)(2,1)} %do_in.1), custom_call_target="tpu_custom_call" | custom-call | tf_op jit(solution)/shard_map/pallas_call | solution.py:463
  31.5 0.8 %shard_map.85 = (bf16[256,512]{1,0:T(8,128)(2,1)}, bf16[256,512]{1,0:T(8,128)(2,1)}, f32[32,256]{1,0:T(8,128)}, f32[32,256]{1,0:T(8,128)}) custom-call(bf16[256,512]{1,0:T(8,128)(2,1)S(1)} %get-tuple-element.8.refs_0_, bf16[256,512]{1,0:T(8,128)(2,1)S(1)} %get-tuple-element.9.refs_1_, f32[32,256]{1,0:T(8,128)S(1)} %get-tuple-element.10.refs_2_, ...), custom_call_target="tpu_custom_call" | custom-call | tf_op jit(solution)/shard_map/pallas_call | solution.py:502
